TPU v7x, 32 devices: a whole 2x2x4 slice. The times are simulated.
32 devices in a mesh: tm: 4 (over y, core), height: 8 (over z, x).
Axes of the slice: x: 2, y: 2, z: 4, core: 2. Of those that a mesh axis runs over, the one named last changes fastest.
Arguments:
- hidden_in: bfloat16 [8, 64, 128, 192], P('tm', 'height'), may hold values from -6 to 6
- gain_first: float32 [192], replicated, may hold values from 0.5 to 2
- weight_first: bfloat16 [3, 3, 3, 192, 192], replicated, may hold values from -0.078125 to 0.078125
- bias_first: float32 [192], replicated, may hold values from -3 to 3
- gain_second: float32 [192], replicated, may hold values from 0.5 to 2
- weight_second: bfloat16 [3, 3, 3, 192, 192], replicated, may hold values from -0.078125 to 0.078125
- bias_second: float32 [192], replicated, may hold values from -3 to 3
Outputs:
- block_out: bfloat16 [8, 64, 128, 192], P('tm', 'height')
All inputs are finite; a program needn't handle non-finite values.
Results may differ from a plain program's by a relative error of at most 0.0042.
Values may be sent and summed in bfloat16 or wider, within the bound.
A program may use at most 64 MiB of HBM per device.

v0:
```python
import jax
import jax.numpy as jnp
from jax import lax
from jax.sharding import PartitionSpec as P

epsilon = 1e-06


def shifted(value, axis, steps):
    count = lax.axis_size(axis)
    leading, last = (max(0, -steps), min(count, count - steps))
    return lax.ppermute(value, axis, [(source, source + steps) for source in range(leading, last)])


def with_halo(value, sides, width):
    for axis, dim in sides:
        size, length = (lax.axis_size(axis), value.shape[dim])
        up = [(i, (i + 1) % size) for i in range(size - 1)]
        down = [(j, i) for i, j in up]
        last = lax.slice_in_dim(value, length - width, length, axis=dim)
        leading = lax.slice_in_dim(value, 0, width, axis=dim)
        before = lax.ppermute(last, axis, up)
        after = lax.ppermute(leading, axis, down)
        value = jnp.concatenate([before, value, after], axis=dim)
    return value


def normalize(values, gain):
    values = values.astype(jnp.float32)
    scaled = values * lax.rsqrt(jnp.mean(values * values, axis=-1, keepdims=True) + epsilon) * gain
    return jax.nn.silu(scaled).astype(jnp.bfloat16)


def apply_taps(extended, weight, bias):
    summed = lax.conv_general_dilated(
        extended[None],
        weight,
        (1, 1, 1),
        ((0, 0), (0, 0), (1, 1)),
        dimension_numbers=("NDHWC", "DHWIO", "NDHWC"),
        preferred_element_type=jnp.float32,
    )
    return summed[0] + bias


def local(hidden_in, gain_first, weight_first, bias_first, gain_second, weight_second, bias_second):
    first_act = normalize(hidden_in, gain_first)
    earlier = shifted(first_act, "tm", 1)
    extended = jnp.concatenate([earlier, first_act], axis=0)
    padded = with_halo(extended, (("height", 1),), 1)
    middle = apply_taps(padded, weight_first, bias_first)
    second_act = normalize(middle, gain_second)
    earlier_mid = shifted(second_act[-2:], "tm", 1)
    extended_mid = jnp.concatenate([earlier_mid, second_act], axis=0)
    padded_mid = with_halo(extended_mid, (("height", 1),), 1)
    branch = apply_taps(padded_mid, weight_second, bias_second)
    return (hidden_in.astype(jnp.float32) + branch).astype(jnp.bfloat16)


def solution(mesh):
    in_specs = (P("tm", "height", None, None), P(), P(), P(), P(), P(), P())
    out_specs = P("tm", "height", None, None)
    return jax.shard_map(local, mesh=mesh, in_specs=in_specs, out_specs=out_specs, check_vma=False)
```

profile of v0, /device:TPU:12, one launch (start us, length us, event | category | flops | bytes accessed | tf_op | source)
XLA Modules:
  0.0 140.6 jit_solution(14219076913884633858)
XLA Ops:
  0.0 2.8 %copy.60 = bf16[2,8,128,192]{3,1,2,0:T(8,128)(2,1)} copy(bf16[2,8,128,192]{2,3,1,0:T(8,128)(2,1)} %param.7) | data formatting | bytes 1572864 | tf_op args[0]
  4.6 2.9 %fusion.23 = bf16[2,8,128,192]{3,1,2,0:T(8,128)(2,1)} fusion(bf16[2,8,128,192]{3,1,2,0:T(8,128)(2,1)} %copy.60, f32[192]{0:T(256)S(1)} %copy-done.8, f32[2,8,128]{1,2,0:T(8,128)S(1)} %copy.62), kind=kLoop, calls=%fused_computation.35 | loop fusion | flops 3145728 | bytes 1581824 | tf_op jit(solution)/shard_map/convert_element_type | solution.py:31
  12.0 11.6 %collective-permute-done = bf16[2,8,128,192]{2,3,1,0:T(8,128)(2,1)S(1)} collective-permute-done((bf16[2,8,128,192]{2,3,1,0:T(8,128)(2,1)}, bf16[2,8,128,192]{2,3,1,0:T(8,128)(2,1)S(1)}, u32[]{:S(2)}, u32[]{:S(2)}) %collective-permute-start) | collective-permute-done | bytes 786464 | tf_op jit(solution)/shard_map/ppermute | solution.py:12
  25.2 4.0 %fusion.37 = (bf16[4,1,128,192]{3,1,2,0:T(2,128)(2,1)}, bf16[4,1,128,192]{3,1,2,0:T(2,128)(2,1)}) fusion(bf16[2,8,128,192]{3,1,2,0:T(8,128)(2,1)} %copy.64, bf16[2,8,128,192]{3,1,2,0:T(8,128)(2,1)} %fusion.23), kind=kLoop, calls=%fused_computation.51 | loop fusion | flops 196608 | bytes 1966080 | tf_op jit(solution)/shard_map/concatenate | solution.py:49
  29.2 3.4 %collective-permute-start.1 = (bf16[4,1,128,192]{3,1,2,0:T(2,128)(2,1)}, bf16[4,1,128,192]{3,1,2,0:T(2,128)(2,1)S(1)}, u32[]{:S(2)}, u32[]{:S(2)}) collective-permute-start(bf16[4,1,128,192]{3,1,2,0:T(2,128)(2,1)} %get-tuple-element.7), channel_id=1, source_target_pairs={{0,1},{1,2},{2,3},{3,4},{4,5},{5,6},{6,7},{8,9},{9,10},{10,11},{11... | collective-permute-start | bytes 589832 | tf_op jit(solution)/shard_map/ppermute | solution.py:22
  32.6 3.3 %collective-permute-start.2 = (bf16[4,1,128,192]{3,1,2,0:T(2,128)(2,1)}, bf16[4,1,128,192]{3,1,2,0:T(2,128)(2,1)}, u32[]{:S(2)}, u32[]{:S(2)}) collective-permute-start(bf16[4,1,128,192]{3,1,2,0:T(2,128)(2,1)} %get-tuple-element.8), channel_id=1, source_target_pairs={{1,0},{2,1},{3,2},{4,3},{5,4},{6,5},{7,6},{9,8},{10,9},{11,10},{12... | collective-permute-start | bytes 589832 | tf_op jit(solution)/shard_map/ppermute | solution.py:23
  37.7 4.4 %copy.66 = bf16[4,8,128,192]{2,3,1,0:T(8,128)(2,1)} copy(bf16[4,8,128,192]{3,1,2,0:T(8,128)(2,1)} %pad_maximum_fusion) | data formatting | bytes 3145728 | tf_op jit(solution)/shard_map/concatenate | solution.py:49
  42.0 4.3 %collective-permute-done.1 = bf16[4,1,128,192]{3,1,2,0:T(2,128)(2,1)S(1)} collective-permute-done((bf16[4,1,128,192]{3,1,2,0:T(2,128)(2,1)}, bf16[4,1,128,192]{3,1,2,0:T(2,128)(2,1)S(1)}, u32[]{:S(2)}, u32[]{:S(2)}) %collective-permute-start.1) | collective-permute-done | bytes 196640 | tf_op jit(solution)/shard_map/ppermute | solution.py:22
  49.5 2.9 %maximum_bitcast_fusion = bf16[4,10,1,128,192]{3,4,1,0,2:T(8,128)(2,1)} fusion(bf16[4,1,128,192]{2,3,1,0:T(8,128)(2,1)S(1)} %copy.67, bf16[4,8,128,192]{2,3,1,0:T(8,128)(2,1)} %copy.66, bf16[4,1,128,192]{2,3,1,0:T(8,128)(2,1)S(1)} %copy.65), kind=kLoop, calls=%fused_computation.43 | loop fusion | flops 1966080 | bytes 3932160 | tf_op jit(solution)/shard_map/broadcast_in_dim | solution.py:36
  52.4 5.1 %copy.84 = bf16[4,10,1,128,192]{4,0,3,1,2:T(4,128)(2,1)} copy(bf16[4,10,1,128,192]{3,4,1,0,2:T(8,128)(2,1)} %maximum_bitcast_fusion) | data formatting | bytes 3932160
  57.5 3.1 %pad.clone = bf16[4,10,1,136,192]{4,0,3,1,2:T(4,128)(2,1)S(1)} pad(bf16[4,10,1,128,192]{4,0,3,1,2:T(4,128)(2,1)} %copy.84, bf16[]{:T(256)} %constant.13), padding=0_0x0_0x0_0x1_7x0_0 | pad | bytes 4055042 | tf_op jit(solution)/shard_map/broadcast_in_dim | solution.py:36
  61.3 6.6 %fusion.32 = f32[2,8,8,17,192]{4,2,3,1,0:T(8,128)S(1)} fusion(bf16[3,3,3,192,192]{4,3,2,1,0:T(8,128)(2,1)S(1)} %copy-done, bf16[4,10,1,7,2,192]{5,3,4,1,0,2:T(8,128)(2,1)S(1)} %slice.24, bf16[4,10,1,8,17,192]{5,3,4,1,0,2:T(8,128)(2,1)S(1)} %copy.70, pred[8,17]{0,1:T(8,128)(4,1)S(1)} %copy-done.12), kind=kOutput, calls=%fused_computation.48 | convolution fusion | flops 4339089408 | bytes 5965960 | tf_op jit(solution)/shard_map/conv_general_dilated | solution.py:35
  70.6 3.2 %multiply_convert_fusion = bf16[2,8,128,192]{3,1,2,0:T(8,128)(2,1)} fusion(f32[2,8,1,136,192]{4,1,3,0,2:T(8,128)} %bitcast.35, f32[192]{0:T(256)S(1)} %copy-done.9, f32[2,8,128]{1,2,0:T(8,128)S(1)} %copy.73, f32[192]{0:T(256)S(1)} %copy-done.7), kind=kLoop, calls=%fused_computation.41 | loop fusion | flops 3145728 | bytes 2369024 | tf_op jit(solution)/shard_map/convert_element_type | solution.py:31
  73.9 2.6 %copy.74 = bf16[2,8,128,192]{2,3,1,0:T(8,128)(2,1)} copy(bf16[2,8,128,192]{3,1,2,0:T(8,128)(2,1)} %multiply_convert_fusion) | data formatting | bytes 1572864 | tf_op jit(solution)/shard_map/convert_element_type | solution.py:31
  78.4 11.6 %collective-permute-done.3 = bf16[2,8,128,192]{2,3,1,0:T(8,128)(2,1)S(1)} collective-permute-done((bf16[2,8,128,192]{2,3,1,0:T(8,128)(2,1)}, bf16[2,8,128,192]{2,3,1,0:T(8,128)(2,1)S(1)}, u32[]{:S(2)}, u32[]{:S(2)}) %collective-permute-start.3) | collective-permute-done | bytes 786464 | tf_op jit(solution)/shard_map/ppermute | solution.py:12
  91.6 4.0 %fusion.35 = (bf16[4,1,128,192]{3,1,2,0:T(2,128)(2,1)}, bf16[4,1,128,192]{3,1,2,0:T(2,128)(2,1)}) fusion(bf16[2,8,128,192]{3,1,2,0:T(8,128)(2,1)} %copy.75, bf16[2,8,128,192]{3,1,2,0:T(8,128)(2,1)} %multiply_convert_fusion), kind=kLoop, calls=%fused_computation.49 | loop fusion | flops 196608 | bytes 1966080 | tf_op jit(solution)/shard_map/concatenate | solution.py:54
  95.6 2.7 %collective-permute-start.4 = (bf16[4,1,128,192]{3,1,2,0:T(2,128)(2,1)}, bf16[4,1,128,192]{3,1,2,0:T(2,128)(2,1)S(1)}, u32[]{:S(2)}, u32[]{:S(2)}) collective-permute-start(bf16[4,1,128,192]{3,1,2,0:T(2,128)(2,1)} %get-tuple-element.5), channel_id=1, source_target_pairs={{0,1},{1,2},{2,3},{3,4},{4,5},{5,6},{6,7},{8,9},{9,10},{10,11},{11... | collective-permute-start | bytes 589832 | tf_op jit(solution)/shard_map/ppermute | solution.py:22
  98.4 4.0 %collective-permute-start.5 = (bf16[4,1,128,192]{3,1,2,0:T(2,128)(2,1)}, bf16[4,1,128,192]{3,1,2,0:T(2,128)(2,1)}, u32[]{:S(2)}, u32[]{:S(2)}) collective-permute-start(bf16[4,1,128,192]{3,1,2,0:T(2,128)(2,1)} %get-tuple-element.6), channel_id=1, source_target_pairs={{1,0},{2,1},{3,2},{4,3},{5,4},{6,5},{7,6},{9,8},{10,9},{11,10},{12... | collective-permute-start | bytes 589832 | tf_op jit(solution)/shard_map/ppermute | solution.py:23
  104.1 4.4 %copy.77 = bf16[4,8,128,192]{2,3,1,0:T(8,128)(2,1)} copy(bf16[4,8,128,192]{3,1,2,0:T(8,128)(2,1)} %pad_maximum_fusion.1) | data formatting | bytes 3145728 | tf_op jit(solution)/shard_map/concatenate | solution.py:54
  108.5 3.7 %collective-permute-done.4 = bf16[4,1,128,192]{3,1,2,0:T(2,128)(2,1)S(1)} collective-permute-done((bf16[4,1,128,192]{3,1,2,0:T(2,128)(2,1)}, bf16[4,1,128,192]{3,1,2,0:T(2,128)(2,1)S(1)}, u32[]{:S(2)}, u32[]{:S(2)}) %collective-permute-start.4) | collective-permute-done | bytes 196640 | tf_op jit(solution)/shard_map/ppermute | solution.py:22
  115.9 2.9 %maximum_bitcast_fusion.1 = bf16[4,10,1,128,192]{3,4,1,0,2:T(8,128)(2,1)} fusion(bf16[4,1,128,192]{2,3,1,0:T(8,128)(2,1)S(1)} %copy.78, bf16[4,8,128,192]{2,3,1,0:T(8,128)(2,1)} %copy.77, bf16[4,1,128,192]{2,3,1,0:T(8,128)(2,1)S(1)} %copy.76), kind=kLoop, calls=%fused_computation.44 | loop fusion | flops 1966080 | bytes 3932160 | tf_op jit(solution)/shard_map/broadcast_in_dim | solution.py:36
  118.9 5.1 %copy.85 = bf16[4,10,1,128,192]{4,0,3,1,2:T(4,128)(2,1)} copy(bf16[4,10,1,128,192]{3,4,1,0,2:T(8,128)(2,1)} %maximum_bitcast_fusion.1) | data formatting | bytes 3932160
  123.9 3.1 %pad.2.clone = bf16[4,10,1,136,192]{4,0,3,1,2:T(4,128)(2,1)S(1)} pad(bf16[4,10,1,128,192]{4,0,3,1,2:T(4,128)(2,1)} %copy.85, bf16[]{:T(256)} %constant.13), padding=0_0x0_0x0_0x1_7x0_0 | pad | bytes 4055042 | tf_op jit(solution)/shard_map/broadcast_in_dim | solution.py:36
  128.8 6.7 %fusion.29 = f32[2,8,8,17,192]{4,2,3,1,0:T(8,128)S(1)} fusion(bf16[3,3,3,192,192]{4,3,2,1,0:T(8,128)(2,1)S(1)} %copy-done.11, bf16[4,10,1,7,2,192]{5,3,4,1,0,2:T(8,128)(2,1)S(1)} %slice.30, bf16[4,10,1,8,17,192]{5,3,4,1,0,2:T(8,128)(2,1)S(1)} %copy.81, pred[8,17]{0,1:T(8,128)(4,1)S(1)} %copy-done.12), kind=kOutput, calls=%fused_computation.47 | convolution fusion | flops 4339089408 | bytes 5965960 | tf_op jit(solution)/shard_map/conv_general_dilated | solution.py:35
  (55 shorter events, 31.9 us)
Async XLA Ops:
  0.0 61.1 %copy-start = (bf16[3,3,3,192,192]{4,3,2,1,0:T(8,128)(2,1)S(1)}, bf16[3,3,3,192,192]{4,3,2,1,0:T(8,128)(2,1)}, u32[]{:S(2)}) copy-start(bf16[3,3,3,192,192]{4,3,2,1,0:T(8,128)(2,1)} %param.9) | copy-start | bytes 5971972
  0.0 4.6 %copy-start.8 = (f32[192]{0:T(256)S(1)}, f32[192]{0:T(256)}, u32[]{:S(2)}) copy-start(f32[192]{0:T(256)} %param.8) | copy-start | bytes 2308
  10.0 13.5 %collective-permute-start = (bf16[2,8,128,192]{2,3,1,0:T(8,128)(2,1)}, bf16[2,8,128,192]{2,3,1,0:T(8,128)(2,1)S(1)}, u32[]{:S(2)}, u32[]{:S(2)}) collective-permute-start(bf16[2,8,128,192]{2,3,1,0:T(8,128)(2,1)} %copy.63), channel_id=1, source_target_pairs={{0,8},{8,16},{16,24},{1,9},{9,17},{17,25},{2,10},{10,18},{18,26},{... | collective-permute-start | bytes 2359304 | tf_op jit(solution)/shard_map/ppermute | solution.py:12
  25.2 10.8 %copy-start.4 = (bf16[2,8,128,192]{3,1,2,0:T(8,128)(2,1)S(1)}, bf16[2,8,128,192]{3,1,2,0:T(8,128)(2,1)}, u32[]{:S(2)}) copy-start(bf16[2,8,128,192]{3,1,2,0:T(8,128)(2,1)} %fusion.23) | copy-start | bytes 2359300
  25.2 10.8 %copy-start.5 = (bf16[2,8,128,192]{3,1,2,0:T(8,128)(2,1)S(1)}, bf16[2,8,128,192]{3,1,2,0:T(8,128)(2,1)}, u32[]{:S(2)}) copy-start(bf16[2,8,128,192]{3,1,2,0:T(8,128)(2,1)} %copy.64) | copy-start | bytes 2359300
  29.2 17.2 %collective-permute-start.1 = (bf16[4,1,128,192]{3,1,2,0:T(2,128)(2,1)}, bf16[4,1,128,192]{3,1,2,0:T(2,128)(2,1)S(1)}, u32[]{:S(2)}, u32[]{:S(2)}) collective-permute-start(bf16[4,1,128,192]{3,1,2,0:T(2,128)(2,1)} %get-tuple-element.7), channel_id=1, source_target_pairs={{0,1},{1,2},{2,3},{3,4},{4,5},{5,6},{6,7},{8,9},{9,10},{10,11},{11... | collective-permute-start | bytes 589832 | tf_op jit(solution)/shard_map/ppermute | solution.py:22
  32.6 15.6 %collective-permute-start.2 = (bf16[4,1,128,192]{3,1,2,0:T(2,128)(2,1)}, bf16[4,1,128,192]{3,1,2,0:T(2,128)(2,1)}, u32[]{:S(2)}, u32[]{:S(2)}) collective-permute-start(bf16[4,1,128,192]{3,1,2,0:T(2,128)(2,1)} %get-tuple-element.8), channel_id=1, source_target_pairs={{1,0},{2,1},{3,2},{4,3},{5,4},{6,5},{7,6},{9,8},{10,9},{11,10},{12... | collective-permute-start | bytes 589832 | tf_op jit(solution)/shard_map/ppermute | solution.py:23
  60.6 0.7 copy-start.12
  68.0 2.1 %copy-start.7 = (f32[192]{0:T(256)S(1)}, f32[192]{0:T(256)}, u32[]{:S(2)}) copy-start(f32[192]{0:T(256)} %param.10) | copy-start | bytes 2308
  68.6 1.4 %copy-start.1 = (f32[2,8,8,17,192]{4,1,3,2,0:T(8,128)}, f32[2,8,8,17,192]{4,1,3,2,0:T(8,128)S(1)}, u32[]{:S(2)}) copy-start(f32[2,8,8,17,192]{4,1,3,2,0:T(8,128)S(1)} %copy.71) | copy-start | bytes 5013508
  68.6 2.0 %copy-start.9 = (f32[192]{0:T(256)S(1)}, f32[192]{0:T(256)}, u32[]{:S(2)}) copy-start(f32[192]{0:T(256)} %param.11) | copy-start | bytes 2308
  76.5 13.5 %collective-permute-start.3 = (bf16[2,8,128,192]{2,3,1,0:T(8,128)(2,1)}, bf16[2,8,128,192]{2,3,1,0:T(8,128)(2,1)S(1)}, u32[]{:S(2)}, u32[]{:S(2)}) collective-permute-start(bf16[2,8,128,192]{2,3,1,0:T(8,128)(2,1)} %copy.74), channel_id=1, source_target_pairs={{0,8},{8,16},{16,24},{1,9},{9,17},{17,25},{2,10},{10,18},{18,26},{... | collective-permute-start | bytes 2359304 | tf_op jit(solution)/shard_map/ppermute | solution.py:12
  91.6 10.8 %copy-start.3 = (bf16[2,8,128,192]{3,1,2,0:T(8,128)(2,1)S(1)}, bf16[2,8,128,192]{3,1,2,0:T(8,128)(2,1)}, u32[]{:S(2)}) copy-start(bf16[2,8,128,192]{3,1,2,0:T(8,128)(2,1)} %multiply_convert_fusion) | copy-start | bytes 2359300
  91.6 10.8 %copy-start.6 = (bf16[2,8,128,192]{3,1,2,0:T(8,128)(2,1)S(1)}, bf16[2,8,128,192]{3,1,2,0:T(8,128)(2,1)}, u32[]{:S(2)}) copy-start(bf16[2,8,128,192]{3,1,2,0:T(8,128)(2,1)} %copy.75) | copy-start | bytes 2359300
  95.6 16.5 %collective-permute-start.4 = (bf16[4,1,128,192]{3,1,2,0:T(2,128)(2,1)}, bf16[4,1,128,192]{3,1,2,0:T(2,128)(2,1)S(1)}, u32[]{:S(2)}, u32[]{:S(2)}) collective-permute-start(bf16[4,1,128,192]{3,1,2,0:T(2,128)(2,1)} %get-tuple-element.5), channel_id=1, source_target_pairs={{0,1},{1,2},{2,3},{3,4},{4,5},{5,6},{6,7},{8,9},{9,10},{10,11},{11... | collective-permute-start | bytes 589832 | tf_op jit(solution)/shard_map/ppermute | solution.py:22
  98.4 16.3 %collective-permute-start.5 = (bf16[4,1,128,192]{3,1,2,0:T(2,128)(2,1)}, bf16[4,1,128,192]{3,1,2,0:T(2,128)(2,1)}, u32[]{:S(2)}, u32[]{:S(2)}) collective-permute-start(bf16[4,1,128,192]{3,1,2,0:T(2,128)(2,1)} %get-tuple-element.6), channel_id=1, source_target_pairs={{1,0},{2,1},{3,2},{4,3},{5,4},{6,5},{7,6},{9,8},{10,9},{11,10},{12... | collective-permute-start | bytes 589832 | tf_op jit(solution)/shard_map/ppermute | solution.py:23
  127.0 1.8 %copy-start.11 = (bf16[3,3,3,192,192]{4,3,2,1,0:T(8,128)(2,1)S(1)}, bf16[3,3,3,192,192]{4,3,2,1,0:T(8,128)(2,1)}, u32[]{:S(2)}) copy-start(bf16[3,3,3,192,192]{4,3,2,1,0:T(8,128)(2,1)} %param.12) | copy-start | bytes 5971972
  135.5 1.2 copy-start.2
  135.5 1.2 copy-start.10
where the time goes:
time: 142 us; the launch traced here: 141 us
  local copies, waits for them, and re-layouts  48.2 us (34%)
  waiting for transfers between devices  34.9 us (25%)
  other arithmetic  26.6 us (19%)
  starting transfers between devices  17.3 us (12%)
  matrix products  13.4 us (9%)
    ppermute x2, waiting for transfers between devices, shifted(): lax.ppermute(value, axis, [(source, source + steps) for source in range(l...  23.2 us
    unnamed x29, local copies, waits for them, and re-layouts  16.4 us
    conv_general_dilated x2, matrix products, apply_taps(): lax.conv_general_dilated(extended[None], weight, (1, 1, 1), ((0, 0), (0,...  13.4 us
    ppermute x2, waiting for transfers between devices, with_halo(): before = lax.ppermute(last, axis, up)  7.97 us
    ppermute x2, starting transfers between devices, with_halo(): after = lax.ppermute(leading, axis, down)  7.34 us
    broadcast_in_dim x2, local copies, waits for them, and re-layouts, apply_taps(): extended[None]  6.2 us
    ppermute x2, starting transfers between devices, with_halo(): before = lax.ppermute(last, axis, up)  6.12 us
    convert_element_type x2, other arithmetic, normalize(): return jax.nn.silu(scaled).astype(jnp.bfloat16)  6.1 us
  transfers between devices with their start and end apart: 6, of which 6 were waited for; matrix products, arithmetic and copies ran while one was open for 9% of the time, Pallas kernels for 0%

commit v1 on v0

v1 whole, which is shorter than its diff:
```python
import functools

import jax
import jax.numpy as jnp
from jax import lax
from jax.experimental import pallas as pl
from jax.experimental.pallas import tpu as pltpu
from jax.sharding import PartitionSpec as P

epsilon = 1e-06
MESH = pl.DeviceIdType.MESH
CHUNK = 4


def normalize(values, gain):
    scaled = values * lax.rsqrt(jnp.mean(values * values, axis=-1, keepdims=True) + epsilon) * gain
    return jax.nn.silu(scaled).astype(jnp.bfloat16)


def kernel(
    tms, heights, x_ref, g1_ref, b1_ref, g2_ref, b2_ref, w1_hbm, w2_hbm, o_ref,
    ext1, ext2, acc, w1, w2, wsem, t_send, t_recv, h_send, h_recv,
):
    frames, rows, width, chans = x_ref.shape
    chunks = rows // CHUNK
    tm, ht = lax.axis_index("tm"), lax.axis_index("height")
    has_prev, has_next = tm > 0, tm < tms - 1
    has_up, has_down = ht > 0, ht < heights - 1

    load1 = pltpu.make_async_copy(w1_hbm, w1, wsem.at[0])
    load2 = pltpu.make_async_copy(w2_hbm, w2, wsem.at[1])
    load1.start()
    load2.start()

    barrier = pltpu.get_barrier_semaphore()
    sides = ((has_prev, {"tm": tm - 1}), (has_next, {"tm": tm + 1}), (has_up, {"height": ht - 1}), (has_down, {"height": ht + 1}))
    for there, who in sides:
        @pl.when(there)
        def _(who=who):
            pl.semaphore_signal(barrier, inc=1, device_id=who, device_id_type=MESH)

    zeros_row = jnp.zeros((width, chans), jnp.bfloat16)
    for ext in (ext1, ext2):
        @pl.when(jnp.logical_not(has_prev))
        def _(ext=ext):
            for f in range(2):
                @pl.loop(0, rows + 2)
                def _(r, f=f):
                    ext[f, r] = zeros_row

        @pl.when(jnp.logical_not(has_up))
        def _(ext=ext):
            for f in range(frames + 2):
                ext[f, 0] = zeros_row

        @pl.when(jnp.logical_not(has_down))
        def _(ext=ext):
            for f in range(frames + 2):
                ext[f, rows + 1] = zeros_row

    pl.semaphore_wait(barrier, sum(there.astype(jnp.int32) for there, _ in sides))

    exts = (ext1, ext2)

    def time_copy(p, f, c):
        lines = pl.ds(1 + c * CHUNK, CHUNK)
        return pltpu.make_async_remote_copy(
            src_ref=exts[p].at[frames + f, lines], dst_ref=exts[p].at[f, lines],
            send_sem=t_send.at[p, f, c], recv_sem=t_recv.at[p, f, c],
            device_id={"tm": tm + 1}, device_id_type=MESH)

    def row_copy(p, f, down):
        src, dst, who = (rows, 0, ht + 1) if down else (1, rows + 1, ht - 1)
        return pltpu.make_async_remote_copy(
            src_ref=exts[p].at[f, src], dst_ref=exts[p].at[f, dst],
            send_sem=h_send.at[p, f, int(down)], recv_sem=h_recv.at[p, f, int(down)],
            device_id={"height": who}, device_id_type=MESH)

    def when_start(cond, copy):
        @pl.when(cond)
        def _():
            copy.start()

    def when_recv(cond, copy):
        @pl.when(cond)
        def _():
            copy.wait_recv()

    def when_sent(cond, copy):
        @pl.when(cond)
        def _():
            copy.wait_send()

    def send_part(p, f, c):
        if c == 0:
            when_start(has_up, row_copy(p, f + 2, False))
        if c == chunks - 1:
            when_start(has_down, row_copy(p, f + 2, True))
        if f >= frames - 2:
            when_start(has_next, time_copy(p, f - (frames - 2), c))

    def contrib(ext, w, o, taps, first):
        @pl.loop(0, chunks)
        def _(c):
            r0 = c * CHUNK
            for k in range(3):
                total = None
                for t in taps:
                    for j in range(3):
                        lines = ext[o + t, pl.ds(r0 + j, CHUNK)].reshape(CHUNK * width, chans)
                        part = jnp.dot(lines, w[t, j, k], preferred_element_type=jnp.float32)
                        total = part if total is None else total + part
                total = total.reshape(CHUNK, width, chans)
                if first:
                    acc[k, o, pl.ds(r0, CHUNK)] = total
                else:
                    acc[k, o, pl.ds(r0, CHUNK)] += total

    at_col = lax.broadcasted_iota(jnp.int32, (width, chans), 0)

    def combined(o, r, bias):
        left = jnp.where(at_col == 0, 0.0, pltpu.roll(acc[0, o, r], 1, 0))
        right = jnp.where(at_col == width - 1, 0.0, pltpu.roll(acc[2, o, r], width - 1, 0))
        return acc[1, o, r] + left + right + bias

    def convolve(p, w, finish):
        ext = exts[p]
        for f in range(2, frames + 2):
            when_recv(has_up, row_copy(p, f, True))
            when_recv(has_down, row_copy(p, f, False))
        for o in range(frames):
            contrib(ext, w, o, tuple(t for t in range(3) if o + t >= 2), True)
        for f in range(2):
            for c in range(chunks):
                when_recv(has_prev, time_copy(p, f, c))
                if c == 0:
                    when_start(has_prev & has_up, row_copy(p, f, False))
                if c == chunks - 1:
                    when_start(has_prev & has_down, row_copy(p, f, True))
        for f in range(2):
            when_recv(has_prev & has_up, row_copy(p, f, True))
            when_recv(has_prev & has_down, row_copy(p, f, False))
        for o in range(min(frames, 2)):
            contrib(ext, w, o, tuple(t for t in range(3) if o + t < 2), False)
        for c in range(chunks):
            for o in range(frames):
                finish(o, c)

    for c in range(chunks):
        for f in range(frames):
            @pl.loop(c * CHUNK, (c + 1) * CHUNK)
            def _(r, f=f):
                ext1[f + 2, r + 1] = normalize(x_ref[f, r].astype(jnp.float32), g1_ref[...])
            send_part(0, f, c)

    def finish_first(o, c):
        @pl.loop(c * CHUNK, (c + 1) * CHUNK)
        def _(r):
            ext2[o + 2, r + 1] = normalize(combined(o, r, b1_ref[...]), g2_ref[...])
        send_part(1, o, c)

    def finish_second(o, c):
        @pl.loop(c * CHUNK, (c + 1) * CHUNK)
        def _(r):
            o_ref[o, r] = (x_ref[o, r].astype(jnp.float32) + combined(o, r, b2_ref[...])).astype(jnp.bfloat16)

    load1.wait()
    convolve(0, w1, finish_first)
    load2.wait()
    convolve(1, w2, finish_second)

    for p in range(2):
        for f in range(2):
            for c in range(chunks):
                when_sent(has_next, time_copy(p, f, c))
        for f in range(frames + 2):
            extra = has_prev if f < 2 else True
            when_sent(has_up & extra, row_copy(p, f, False))
            when_sent(has_down & extra, row_copy(p, f, True))


def local(tms, heights, hidden_in, gain_first, weight_first, bias_first, gain_second, weight_second, bias_second):
    frames, rows, width, chans = hidden_in.shape
    chunks = rows // CHUNK
    vmem = pl.BlockSpec(memory_space=pltpu.VMEM)
    hbm = pl.BlockSpec(memory_space=pl.ANY)
    ext = pltpu.VMEM((frames + 2, rows + 2, width, chans), jnp.bfloat16)
    weight = pltpu.VMEM(weight_first.shape, jnp.bfloat16)
    dma = pltpu.SemaphoreType.DMA
    flops = 2 * 2 * frames * rows * width * 27 * chans * chans
    return pl.pallas_call(
        functools.partial(kernel, tms, heights),
        out_shape=jax.ShapeDtypeStruct(hidden_in.shape, jnp.bfloat16),
        in_specs=[vmem] * 5 + [hbm] * 2,
        out_specs=vmem,
        scratch_shapes=[
            ext,
            ext,
            pltpu.VMEM((3, frames, rows, width, chans), jnp.float32),
            weight,
            weight,
            dma((2,)),
            dma((2, 2, chunks)),
            dma((2, 2, chunks)),
            dma((2, frames + 2, 2)),
            dma((2, frames + 2, 2)),
        ],
        compiler_params=pltpu.CompilerParams(
            collective_id=0, has_side_effects=True, vmem_limit_bytes=48 * 2**20
        ),
        cost_estimate=pl.CostEstimate(flops=flops, bytes_accessed=8 * 2**20, transcendentals=0),
    )(
        hidden_in,
        gain_first.reshape(1, chans),
        bias_first.reshape(1, chans),
        gain_second.reshape(1, chans),
        bias_second.reshape(1, chans),
        weight_first,
        weight_second,
    )


def solution(mesh):
    in_specs = (P("tm", "height", None, None), P(), P(), P(), P(), P(), P())
    out_specs = P("tm", "height", None, None)
    body = functools.partial(local, mesh.shape["tm"], mesh.shape["height"])
    return jax.shard_map(body, mesh=mesh, in_specs=in_specs, out_specs=out_specs, check_vma=False)
```

time: 142 us -> 57.3 us (0.40)
  Pallas kernels: 0 us -> 49.8 us
  local copies, waits for them, and re-layouts: 48.2 us -> 7.15 us
  waiting for transfers between devices: 34.9 us -> 0 us
  other arithmetic: 26.6 us -> 0 us
  starting transfers between devices: 17.3 us -> 0 us
  matrix products: 13.4 us -> 0 us
    pallas_call x0 -> x1, Pallas kernels: none -> 49.8 us  [local(): pl.pallas_call(functools.partial(kernel, tms, heights), out_shape=jax.Sha...]
    ppermute x6 -> x0, waiting for transfers between devices: 34.9 us -> none  [the longest x2 23.2 us: shifted(): lax.ppermute(value, axis, [(source, source + steps) for source in range(l...]
    ppermute x6 -> x0, starting transfers between devices: 17.3 us -> none  [the longest x2 7.34 us: with_halo(): after = lax.ppermute(leading, axis, down)]
    conv_general_dilated x2 -> x0, matrix products: 13.4 us -> none  [apply_taps(): lax.conv_general_dilated(extended[None], weight, (1, 1, 1), ((0, 0), (0,...]
    concatenate x4 -> x0, other arithmetic: 11.4 us -> none  [the longest x2 5.69 us: local(): extended_mid = jnp.concatenate([earlier_mid, second_act], axis=0)]
    unnamed x29 -> x11, local copies, waits for them, and re-layouts: 16.4 us -> 5.89 us
    concatenate x2 -> x0, local copies, waits for them, and re-layouts: 8.78 us -> none  [the longest x1 4.39 us: local(): extended = jnp.concatenate([earlier, first_act], axis=0)]
    convert_element_type x3 -> x0, local copies, waits for them, and re-layouts: 7.78 us -> none  [the longest x2 5.18 us: normalize(): return jax.nn.silu(scaled).astype(jnp.bfloat16)]
  transfers between devices with their start and end apart: 6 -> 0, of which waited for: 6 -> 0; matrix products, arithmetic and copies ran while one was open for 9% -> 0% of each run, Pallas kernels for 0% -> 0%
where the time goes in v1:
time: 57.3 us; the launch traced here: 57 us
  Pallas kernels  49.8 us (87%)
  local copies, waits for them, and re-layouts  7.15 us (12%)
    pallas_call x1, Pallas kernels, local(): pl.pallas_call(functools.partial(kernel, tms, heights), out_shape=jax.Sha...  49.8 us
    unnamed x11, local copies, waits for them, and re-layouts  5.89 us
    pallas_call x1, local copies, waits for them, and re-layouts, local(): pl.pallas_call(functools.partial(kernel, tms, heights), out_shape=jax.Sha...  1.26 us

profile of v1, /device:TPU:12, one launch (start us, length us, event | category | flops | bytes accessed | tf_op | source)
XLA Modules:
  0.0 57.0 jit_solution(6155145441742785840)
XLA Ops:
  0.0 1.4 %copy.8.x_ref = bf16[2,8,128,192]{3,2,1,0:T(8,128)(2,1)S(1)} copy(bf16[2,8,128,192]{2,3,1,0:T(8,128)(2,1)} %param.7) | data formatting | bytes 1572864 | tf_op args[0]
  1.4 0.0 copy-start
  1.5 1.7 %copy-done = bf16[3,3,3,192,192]{4,3,2,1,0:T(8,128)(2,1)S(1)} copy-done((bf16[3,3,3,192,192]{4,3,2,1,0:T(8,128)(2,1)S(1)}, bf16[3,3,3,192,192]{4,3,2,1,0:T(8,128)(2,1)}, u32[]{:S(2)}) %copy-start) | copy-done | bytes 1990680
  3.2 0.0 copy-start.1
  3.2 0.7 %copy-done.1 = f32[192]{0:T(256)S(1)} copy-done((f32[192]{0:T(256)S(1)}, f32[192]{0:T(256)}, u32[]{:S(2)}) %copy-start.1) | copy-done | bytes 792
  3.9 0.0 copy-start.2
  3.9 0.7 %copy-done.2 = f32[192]{0:T(256)S(1)} copy-done((f32[192]{0:T(256)S(1)}, f32[192]{0:T(256)}, u32[]{:S(2)}) %copy-start.2) | copy-done | bytes 792
  4.6 0.0 copy-start.3
  4.6 0.7 %copy-done.3 = f32[192]{0:T(256)S(1)} copy-done((f32[192]{0:T(256)S(1)}, f32[192]{0:T(256)}, u32[]{:S(2)}) %copy-start.3) | copy-done | bytes 792
  5.2 0.0 copy-start.4
  5.2 0.7 %copy-done.4 = f32[192]{0:T(256)S(1)} copy-done((f32[192]{0:T(256)S(1)}, f32[192]{0:T(256)}, u32[]{:S(2)}) %copy-start.4) | copy-done | bytes 792
  5.9 49.8 %shard_map.73 = bf16[2,8,128,192]{3,2,1,0:T(8,128)(2,1)S(1)} custom-call(bf16[2,8,128,192]{3,2,1,0:T(8,128)(2,1)S(1)} %copy.8.x_ref, f32[1,192]{1,0:T(1,128)S(1)} %bitcast.4, f32[1,192]{1,0:T(1,128)S(1)} %bitcast.5, f32[1,192]{1,0:T(1,128)S(1)} %bitcast.6, f32[1,192]{1,0:T(1,128)S(1)} %bitcast.7, bf16[3,3,3,192,192]{4,3,2,1,0:T(8,128)(2,1)S(1)} %copy-done, ...), custom_call_target="tpu_custom_call" | custom-call | flops 8153726976 | bytes 8388608 | tf_op jit(solution)/shard_map/pallas_call | solution.py:191
  55.8 1.3 %copy.9 = bf16[2,8,128,192]{2,3,1,0:T(8,128)(2,1)} copy(bf16[2,8,128,192]{3,2,1,0:T(8,128)(2,1)S(1)} %shard_map.73) | data formatting | bytes 1572864 | tf_op jit(solution)/shard_map/pallas_call | solution.py:191
Async XLA Ops:
  1.4 1.8 %copy-start = (bf16[3,3,3,192,192]{4,3,2,1,0:T(8,128)(2,1)S(1)}, bf16[3,3,3,192,192]{4,3,2,1,0:T(8,128)(2,1)}, u32[]{:S(2)}) copy-start(bf16[3,3,3,192,192]{4,3,2,1,0:T(8,128)(2,1)} %w1_hbm.1) | copy-start | bytes 5971972
  3.2 0.7 %copy-start.1 = (f32[192]{0:T(256)S(1)}, f32[192]{0:T(256)}, u32[]{:S(2)}) copy-start(f32[192]{0:T(256)} %param.8) | copy-start | bytes 2308
  3.9 0.7 %copy-start.2 = (f32[192]{0:T(256)S(1)}, f32[192]{0:T(256)}, u32[]{:S(2)}) copy-start(f32[192]{0:T(256)} %param.10) | copy-start | bytes 2308
  4.6 0.7 %copy-start.3 = (f32[192]{0:T(256)S(1)}, f32[192]{0:T(256)}, u32[]{:S(2)}) copy-start(f32[192]{0:T(256)} %param.11) | copy-start | bytes 2308
  5.2 0.7 %copy-start.4 = (f32[192]{0:T(256)S(1)}, f32[192]{0:T(256)}, u32[]{:S(2)}) copy-start(f32[192]{0:T(256)} %param.13) | copy-start | bytes 2308

commit v2 on v1

--- a/solution.py
+++ b/solution.py
@@ -13,15 +13,15 @@
 
 
 def normalize(values, gain):
-    scaled = values * lax.rsqrt(jnp.mean(values * values, axis=-1, keepdims=True) + epsilon) * gain
+    scaled = values * lax.rsqrt(jnp.mean(values * values, axis=0, keepdims=True) + epsilon) * gain
     return jax.nn.silu(scaled).astype(jnp.bfloat16)
 
 
 def kernel(
     tms, heights, x_ref, g1_ref, b1_ref, g2_ref, b2_ref, w1_hbm, w2_hbm, o_ref,
-    ext1, ext2, acc, w1, w2, wsem, t_send, t_recv, h_send, h_recv,
+    ext1, ext2, acc, w1, w2, turned, vecs, vsem, wsem, t_send, t_recv, h_send, h_recv,
 ):
-    frames, rows, width, chans = x_ref.shape
+    frames, rows, chans, width = x_ref.shape
     chunks = rows // CHUNK
     tm, ht = lax.axis_index("tm"), lax.axis_index("height")
     has_prev, has_next = tm > 0, tm < tms - 1
@@ -31,6 +31,9 @@
     load2 = pltpu.make_async_copy(w2_hbm, w2, wsem.at[1])
     load1.start()
     load2.start()
+    small = [pltpu.make_async_copy(ref, vecs.at[i], vsem.at[i]) for i, ref in enumerate((g1_ref, b1_ref, g2_ref, b2_ref))]
+    for copy in small:
+        copy.start()
 
     barrier = pltpu.get_barrier_semaphore()
     sides = ((has_prev, {"tm": tm - 1}), (has_next, {"tm": tm + 1}), (has_up, {"height": ht - 1}), (has_down, {"height": ht + 1}))
@@ -39,7 +42,7 @@
         def _(who=who):
             pl.semaphore_signal(barrier, inc=1, device_id=who, device_id_type=MESH)
 
-    zeros_row = jnp.zeros((width, chans), jnp.bfloat16)
+    zeros_row = jnp.zeros((chans, width), jnp.bfloat16)
     for ext in (ext1, ext2):
         @pl.when(jnp.logical_not(has_prev))
         def _(ext=ext):
@@ -99,37 +102,49 @@
         if f >= frames - 2:
             when_start(has_next, time_copy(p, f - (frames - 2), c))
 
-    def contrib(ext, w, o, taps, first):
+    def turn(w):
+        square = (chans, chans)
+        same = lax.broadcasted_iota(jnp.int32, square, 0) == lax.broadcasted_iota(jnp.int32, square, 1)
+        identity = same.astype(jnp.float32).astype(jnp.bfloat16)
+
+        @pl.loop(0, 3)
+        def _(t):
+            for k in range(3):
+                taps = jnp.concatenate([w[t, j, k] for j in range(3)], axis=0)
+                flipped = lax.dot_general(identity, taps, (((1,), (1,)), ((), ())), preferred_element_type=jnp.float32)
+                turned[t, k * chans:(k + 1) * chans, :] = flipped.astype(jnp.bfloat16)
+
+    def contrib(ext, o, taps, first):
         @pl.loop(0, chunks)
         def _(c):
             r0 = c * CHUNK
-            for k in range(3):
-                total = None
-                for t in taps:
-                    for j in range(3):
-                        lines = ext[o + t, pl.ds(r0 + j, CHUNK)].reshape(CHUNK * width, chans)
-                        part = jnp.dot(lines, w[t, j, k], preferred_element_type=jnp.float32)
-                        total = part if total is None else total + part
-                total = total.reshape(CHUNK, width, chans)
-                if first:
-                    acc[k, o, pl.ds(r0, CHUNK)] = total
-                else:
-                    acc[k, o, pl.ds(r0, CHUNK)] += total
-
-    at_col = lax.broadcasted_iota(jnp.int32, (width, chans), 0)
-
-    def combined(o, r, bias):
-        left = jnp.where(at_col == 0, 0.0, pltpu.roll(acc[0, o, r], 1, 0))
-        right = jnp.where(at_col == width - 1, 0.0, pltpu.roll(acc[2, o, r], width - 1, 0))
-        return acc[1, o, r] + left + right + bias
+            total = None
+            for t in taps:
+                lines = [ext[o + t, r0 + i] for i in range(CHUNK + 2)]
+                block = jnp.concatenate([jnp.concatenate(lines[j:j + CHUNK], axis=1) for j in range(3)], axis=0)
+                part = jnp.dot(turned[t], block, preferred_element_type=jnp.float32)
+                total = part if total is None else total + part
+            if first:
+                acc[o, c] = total
+            else:
+                acc[o, c] += total
+
+    at_col = lax.broadcasted_iota(jnp.int32, (chans, width), 1)
+
+    def combined(o, c, i, bias):
+        cols = slice(i * width, (i + 1) * width)
+        left = jnp.where(at_col == 0, 0.0, pltpu.roll(acc[o, c, 0:chans, cols], 1, 1))
+        right = jnp.where(at_col == width - 1, 0.0, pltpu.roll(acc[o, c, 2 * chans:3 * chans, cols], width - 1, 1))
+        return acc[o, c, chans:2 * chans, cols] + left + right + bias
 
     def convolve(p, w, finish):
         ext = exts[p]
+        turn(w)
         for f in range(2, frames + 2):
             when_recv(has_up, row_copy(p, f, True))
             when_recv(has_down, row_copy(p, f, False))
         for o in range(frames):
-            contrib(ext, w, o, tuple(t for t in range(3) if o + t >= 2), True)
+            contrib(ext, o, tuple(t for t in range(3) if o + t >= 2), True)
         for f in range(2):
             for c in range(chunks):
                 when_recv(has_prev, time_copy(p, f, c))
@@ -141,28 +156,34 @@
             when_recv(has_prev & has_up, row_copy(p, f, True))
             when_recv(has_prev & has_down, row_copy(p, f, False))
         for o in range(min(frames, 2)):
-            contrib(ext, w, o, tuple(t for t in range(3) if o + t < 2), False)
+            contrib(ext, o, tuple(t for t in range(3) if o + t < 2), False)
         for c in range(chunks):
             for o in range(frames):
                 finish(o, c)
 
+    for copy in small:
+        copy.wait()
+    square = (chans, chans)
+    diagonal = lax.broadcasted_iota(jnp.int32, square, 0) == lax.broadcasted_iota(jnp.int32, square, 1)
+    gain1, bias1, gain2, bias2 = [
+        jnp.sum(jnp.where(diagonal, vecs[i], 0.0), axis=1, keepdims=True) for i in range(4)
+    ]
     for c in range(chunks):
         for f in range(frames):
             @pl.loop(c * CHUNK, (c + 1) * CHUNK)
             def _(r, f=f):
-                ext1[f + 2, r + 1] = normalize(x_ref[f, r].astype(jnp.float32), g1_ref[...])
+                ext1[f + 2, r + 1] = normalize(x_ref[f, r].astype(jnp.float32), gain1)
             send_part(0, f, c)
 
     def finish_first(o, c):
-        @pl.loop(c * CHUNK, (c + 1) * CHUNK)
-        def _(r):
-            ext2[o + 2, r + 1] = normalize(combined(o, r, b1_ref[...]), g2_ref[...])
+        for i in range(CHUNK):
+            ext2[o + 2, c * CHUNK + i + 1] = normalize(combined(o, c, i, bias1), gain2)
         send_part(1, o, c)
 
     def finish_second(o, c):
-        @pl.loop(c * CHUNK, (c + 1) * CHUNK)
-        def _(r):
-            o_ref[o, r] = (x_ref[o, r].astype(jnp.float32) + combined(o, r, b2_ref[...])).astype(jnp.bfloat16)
+        for i in range(CHUNK):
+            r = c * CHUNK + i
+            o_ref[o, r] = (x_ref[o, r].astype(jnp.float32) + combined(o, c, i, bias2)).astype(jnp.bfloat16)
 
     load1.wait()
     convolve(0, w1, finish_first)
@@ -184,21 +205,25 @@
     chunks = rows // CHUNK
     vmem = pl.BlockSpec(memory_space=pltpu.VMEM)
     hbm = pl.BlockSpec(memory_space=pl.ANY)
-    ext = pltpu.VMEM((frames + 2, rows + 2, width, chans), jnp.bfloat16)
+    ext = pltpu.VMEM((frames + 2, rows + 2, chans, width), jnp.bfloat16)
     weight = pltpu.VMEM(weight_first.shape, jnp.bfloat16)
     dma = pltpu.SemaphoreType.DMA
     flops = 2 * 2 * frames * rows * width * 27 * chans * chans
-    return pl.pallas_call(
+    turned_in = jnp.swapaxes(hidden_in, 2, 3)
+    result = pl.pallas_call(
         functools.partial(kernel, tms, heights),
-        out_shape=jax.ShapeDtypeStruct(hidden_in.shape, jnp.bfloat16),
-        in_specs=[vmem] * 5 + [hbm] * 2,
+        out_shape=jax.ShapeDtypeStruct(turned_in.shape, jnp.bfloat16),
+        in_specs=[vmem] + [hbm] * 6,
         out_specs=vmem,
         scratch_shapes=[
             ext,
             ext,
-            pltpu.VMEM((3, frames, rows, width, chans), jnp.float32),
+            pltpu.VMEM((frames, chunks, 3 * chans, CHUNK * width), jnp.float32),
             weight,
             weight,
+            pltpu.VMEM((3, 3 * chans, 3 * chans), jnp.bfloat16),
+            pltpu.VMEM((4, 1, chans), jnp.float32),
+            dma((4,)),
             dma((2,)),
             dma((2, 2, chunks)),
             dma((2, 2, chunks)),
@@ -206,11 +231,11 @@
             dma((2, frames + 2, 2)),
         ],
         compiler_params=pltpu.CompilerParams(
-            collective_id=0, has_side_effects=True, vmem_limit_bytes=48 * 2**20
+            collective_id=0, has_side_effects=True, vmem_limit_bytes=56 * 2**20
         ),
         cost_estimate=pl.CostEstimate(flops=flops, bytes_accessed=8 * 2**20, transcendentals=0),
     )(
-        hidden_in,
+        turned_in,
         gain_first.reshape(1, chans),
         bias_first.reshape(1, chans),
         gain_second.reshape(1, chans),
@@ -218,6 +243,7 @@
         weight_first,
         weight_second,
     )
+    return jnp.swapaxes(result, 2, 3)
 
 
 def solution(mesh):

time: 57.3 us -> 45 us (0.79)
  Pallas kernels: 49.8 us -> 42.7 us
  local copies, waits for them, and re-layouts: 7.15 us -> 2.07 us
    pallas_call x1, Pallas kernels: 49.8 us -> 42.7 us  [local(): pl.pallas_call(functools.partial(kernel, tms, heights), out_shape=jax.Sha...]
    unnamed x11 -> x1, local copies, waits for them, and re-layouts: 5.89 us -> 2.07 us
    pallas_call x1 -> x0, local copies, waits for them, and re-layouts: 1.26 us -> none  [local(): pl.pallas_call(functools.partial(kernel, tms, heights), out_shape=jax.Sha...]
where the time goes in v2:
time: 45 us; the launch traced here: 44.8 us
  Pallas kernels  42.7 us (95%)
  local copies, waits for them, and re-layouts  2.07 us (5%)
    pallas_call x1, Pallas kernels, local(): pl.pallas_call(functools.partial(kernel, tms, heights), out_shape=jax.Sha...  42.7 us
    unnamed x1, local copies, waits for them, and re-layouts  2.07 us

profile of v2, /device:TPU:12, one launch (start us, length us, event | category | flops | bytes accessed | tf_op | source)
XLA Modules:
  0.0 44.8 jit_solution(8145423975161400720)
XLA Ops:
  0.0 42.7 %shard_map.73 = bf16[2,8,192,128]{3,2,1,0:T(8,128)(2,1)} custom-call(bf16[2,8,192,128]{3,2,1,0:T(8,128)(2,1)} %bitcast.7, f32[1,192]{1,0:T(1,128)} %bitcast.8, f32[1,192]{1,0:T(1,128)} %bitcast.9, f32[1,192]{1,0:T(1,128)} %bitcast.10, f32[1,192]{1,0:T(1,128)} %bitcast.11, bf16[3,3,3,192,192]{4,3,2,1,0:T(8,128)(2,1)} %w1_hbm.1, ...), custom_call_target="tpu_custom_call" | custom-call | flops 8153726976 | bytes 8388608 | tf_op jit(solution)/shard_map/pallas_call | solution.py:213
  42.7 2.1 %copy.9 = bf16[2,8,128,192]{2,3,1,0:T(8,128)(2,1)} copy(bf16[2,8,128,192]{2,3,1,0:T(8,128)(2,1)} %bitcast.6) | data formatting | bytes 1572864

commit v3 on v2

--- a/solution.py
+++ b/solution.py
@@ -30,7 +30,6 @@
     load1 = pltpu.make_async_copy(w1_hbm, w1, wsem.at[0])
     load2 = pltpu.make_async_copy(w2_hbm, w2, wsem.at[1])
     load1.start()
-    load2.start()
     small = [pltpu.make_async_copy(ref, vecs.at[i], vsem.at[i]) for i, ref in enumerate((g1_ref, b1_ref, g2_ref, b2_ref))]
     for copy in small:
         copy.start()
@@ -61,7 +60,6 @@
             for f in range(frames + 2):
                 ext[f, rows + 1] = zeros_row
 
-    pl.semaphore_wait(barrier, sum(there.astype(jnp.int32) for there, _ in sides))
 
     exts = (ext1, ext2)
 
@@ -102,7 +100,7 @@
         if f >= frames - 2:
             when_start(has_next, time_copy(p, f - (frames - 2), c))
 
-    def turn(w):
+    def turn(p, w):
         square = (chans, chans)
         same = lax.broadcasted_iota(jnp.int32, square, 0) == lax.broadcasted_iota(jnp.int32, square, 1)
         identity = same.astype(jnp.float32).astype(jnp.bfloat16)
@@ -112,54 +110,53 @@
             for k in range(3):
                 taps = jnp.concatenate([w[t, j, k] for j in range(3)], axis=0)
                 flipped = lax.dot_general(identity, taps, (((1,), (1,)), ((), ())), preferred_element_type=jnp.float32)
-                turned[t, k * chans:(k + 1) * chans, :] = flipped.astype(jnp.bfloat16)
-
-    def contrib(ext, o, taps, first):
-        @pl.loop(0, chunks)
-        def _(c):
-            r0 = c * CHUNK
-            total = None
-            for t in taps:
-                lines = [ext[o + t, r0 + i] for i in range(CHUNK + 2)]
-                block = jnp.concatenate([jnp.concatenate(lines[j:j + CHUNK], axis=1) for j in range(3)], axis=0)
-                part = jnp.dot(turned[t], block, preferred_element_type=jnp.float32)
-                total = part if total is None else total + part
-            if first:
-                acc[o, c] = total
-            else:
-                acc[o, c] += total
+                turned[p, t, k * chans:(k + 1) * chans, :] = flipped.astype(jnp.bfloat16)
+
+    def contrib(p, o, taps, first):
+        ext, total = exts[p], None
+        for t in taps:
+            lines = [ext[o + t, i] for i in range(rows + 2)]
+            block = jnp.concatenate([jnp.concatenate(lines[j:j + rows], axis=1) for j in range(3)], axis=0)
+            part = jnp.dot(turned[p, t], block, preferred_element_type=jnp.float32)
+            total = part if total is None else total + part
+        if first:
+            acc[o] = total
+        else:
+            acc[o] += total
 
     at_col = lax.broadcasted_iota(jnp.int32, (chans, width), 1)
 
-    def combined(o, c, i, bias):
-        cols = slice(i * width, (i + 1) * width)
-        left = jnp.where(at_col == 0, 0.0, pltpu.roll(acc[o, c, 0:chans, cols], 1, 1))
-        right = jnp.where(at_col == width - 1, 0.0, pltpu.roll(acc[o, c, 2 * chans:3 * chans, cols], width - 1, 1))
-        return acc[o, c, chans:2 * chans, cols] + left + right + bias
-
-    def convolve(p, w, finish):
-        ext = exts[p]
-        turn(w)
+    def combined(o, r, bias):
+        cols = slice(r * width, (r + 1) * width)
+        left = jnp.where(at_col == 0, 0.0, pltpu.roll(acc[o, 0:chans, cols], 1, 1))
+        right = jnp.where(at_col == width - 1, 0.0, pltpu.roll(acc[o, 2 * chans:3 * chans, cols], width - 1, 1))
+        return acc[o, chans:2 * chans, cols] + left + right + bias
+
+    def convolve(p, finish, meanwhile=None):
         for f in range(2, frames + 2):
             when_recv(has_up, row_copy(p, f, True))
             when_recv(has_down, row_copy(p, f, False))
         for o in range(frames):
-            contrib(ext, o, tuple(t for t in range(3) if o + t >= 2), True)
-        for f in range(2):
+            contrib(p, o, tuple(t for t in range(3) if o + t >= 2), True)
+        if meanwhile is not None:
+            meanwhile()
+        for o in range(2, frames):
+            for c in range(chunks):
+                finish(o, c)
+        for f in (1, 0):
             for c in range(chunks):
                 when_recv(has_prev, time_copy(p, f, c))
                 if c == 0:
                     when_start(has_prev & has_up, row_copy(p, f, False))
                 if c == chunks - 1:
                     when_start(has_prev & has_down, row_copy(p, f, True))
-        for f in range(2):
             when_recv(has_prev & has_up, row_copy(p, f, True))
             when_recv(has_prev & has_down, row_copy(p, f, False))
-        for o in range(min(frames, 2)):
-            contrib(ext, o, tuple(t for t in range(3) if o + t < 2), False)
-        for c in range(chunks):
-            for o in range(frames):
-                finish(o, c)
+            for o in range(f, -1, -1):
+                contrib(p, o, (f - o,), False)
+                if o == f:
+                    for c in range(chunks):
+                        finish(o, c)
 
     for copy in small:
         copy.wait()
@@ -168,27 +165,44 @@
     gain1, bias1, gain2, bias2 = [
         jnp.sum(jnp.where(diagonal, vecs[i], 0.0), axis=1, keepdims=True) for i in range(4)
     ]
-    for c in range(chunks):
-        for f in range(frames):
-            @pl.loop(c * CHUNK, (c + 1) * CHUNK)
-            def _(r, f=f):
-                ext1[f + 2, r + 1] = normalize(x_ref[f, r].astype(jnp.float32), gain1)
+    for f in range(frames):
+        @pl.loop(0, rows)
+        def _(r, f=f):
+            ext1[f + 2, r + 1] = normalize(x_ref[f, r].astype(jnp.float32), gain1)
+
+    pl.semaphore_wait(barrier, sum(there.astype(jnp.int32) for there, _ in sides))
+    for f in range(frames - 1, -1, -1):
+        for c in range(chunks):
             send_part(0, f, c)
 
     def finish_first(o, c):
-        for i in range(CHUNK):
-            ext2[o + 2, c * CHUNK + i + 1] = normalize(combined(o, c, i, bias1), gain2)
+        for r in range(c * CHUNK, (c + 1) * CHUNK):
+            ext2[o + 2, r + 1] = normalize(combined(o, r, bias1), gain2)
         send_part(1, o, c)
 
     def finish_second(o, c):
-        for i in range(CHUNK):
-            r = c * CHUNK + i
-            o_ref[o, r] = (x_ref[o, r].astype(jnp.float32) + combined(o, c, i, bias2)).astype(jnp.bfloat16)
+        for r in range(c * CHUNK, (c + 1) * CHUNK):
+            o_ref[o, r] = (x_ref[o, r].astype(jnp.float32) + combined(o, r, bias2)).astype(jnp.bfloat16)
 
     load1.wait()
-    convolve(0, w1, finish_first)
-    load2.wait()
-    convolve(1, w2, finish_second)
+    load2.start()
+    turn(0, w1)
+    other_chip = has_prev & (lax.rem(tm, 2) == 0)
+
+    def turn_second():
+        load2.wait()
+
+        @pl.when(other_chip)
+        def _():
+            turn(1, w2)
+
+    convolve(0, finish_first, turn_second)
+
+    @pl.when(jnp.logical_not(other_chip))
+    def _():
+        turn(1, w2)
+
+    convolve(1, finish_second)
 
     for p in range(2):
         for f in range(2):
@@ -218,10 +232,10 @@
         scratch_shapes=[
             ext,
             ext,
-            pltpu.VMEM((frames, chunks, 3 * chans, CHUNK * width), jnp.float32),
+            pltpu.VMEM((frames, 3 * chans, rows * width), jnp.float32),
             weight,
             weight,
-            pltpu.VMEM((3, 3 * chans, 3 * chans), jnp.bfloat16),
+            pltpu.VMEM((2, 3, 3 * chans, 3 * chans), jnp.bfloat16),
             pltpu.VMEM((4, 1, chans), jnp.float32),
             dma((4,)),
             dma((2,)),

time: 45 us -> 48.1 us (1.069)
  the two profiles are of different devices: /device:TPU:12 before, /device:TPU:14 now
where the time goes in v3:
time: 48.1 us; the launch traced here: 47.9 us
  Pallas kernels  45.8 us (95%)
  local copies, waits for them, and re-layouts  2.07 us (4%)
    pallas_call x1, Pallas kernels, local(): pl.pallas_call(functools.partial(kernel, tms, heights), out_shape=jax.Sha...  45.8 us
    unnamed x1, local copies, waits for them, and re-layouts  2.07 us

profile of v3, /device:TPU:14, one launch (start us, length us, event | category | flops | bytes accessed | tf_op | source)
XLA Modules:
  0.0 47.9 jit_solution(9412758709654922930)
XLA Ops:
  0.0 45.8 %shard_map.73 = bf16[2,8,192,128]{3,2,1,0:T(8,128)(2,1)} custom-call(bf16[2,8,192,128]{3,2,1,0:T(8,128)(2,1)} %bitcast.7, f32[1,192]{1,0:T(1,128)} %bitcast.8, f32[1,192]{1,0:T(1,128)} %bitcast.9, f32[1,192]{1,0:T(1,128)} %bitcast.10, f32[1,192]{1,0:T(1,128)} %bitcast.11, bf16[3,3,3,192,192]{4,3,2,1,0:T(8,128)(2,1)} %w1_hbm.1, ...), custom_call_target="tpu_custom_call" | custom-call | flops 8153726976 | bytes 8388608 | tf_op jit(solution)/shard_map/pallas_call | solution.py:227
  45.8 2.1 %copy.9 = bf16[2,8,128,192]{2,3,1,0:T(8,128)(2,1)} copy(bf16[2,8,128,192]{2,3,1,0:T(8,128)(2,1)} %bitcast.6) | data formatting | bytes 1572864

commit v4 on v3

--- a/solution.py
+++ b/solution.py
@@ -19,12 +19,14 @@
 
 def kernel(
     tms, heights, x_ref, g1_ref, b1_ref, g2_ref, b2_ref, w1_hbm, w2_hbm, o_ref,
-    ext1, ext2, acc, w1, w2, turned, vecs, vsem, wsem, t_send, t_recv, h_send, h_recv,
+    ext1, ext2, acc, w1, w2, turned, vecs, vsem, wsem, t_send, t_recv, h_send, h_recv, c_send,
 ):
     frames, rows, chans, width = x_ref.shape
     chunks = rows // CHUNK
     tm, ht = lax.axis_index("tm"), lax.axis_index("height")
     has_prev, has_next = tm > 0, tm < tms - 1
+    other_chip = has_prev & (lax.rem(tm, 2) == 0)
+    to_core = has_next & (lax.rem(tm, 2) == 0)
     has_up, has_down = ht > 0, ht < heights - 1
 
     load1 = pltpu.make_async_copy(w1_hbm, w1, wsem.at[0])
@@ -76,6 +78,13 @@
             src_ref=exts[p].at[f, src], dst_ref=exts[p].at[f, dst],
             send_sem=h_send.at[p, f, int(down)], recv_sem=h_recv.at[p, f, int(down)],
             device_id={"height": who}, device_id_type=MESH)
+
+    def corner_copy(p, f, down):
+        line = 0 if down else rows + 1
+        return pltpu.make_async_remote_copy(
+            src_ref=exts[p].at[frames + f, line], dst_ref=exts[p].at[f, line],
+            send_sem=c_send.at[p, f, int(down)], recv_sem=h_recv.at[p, f, int(down)],
+            device_id={"tm": tm + 1}, device_id_type=MESH)
 
     def when_start(cond, copy):
         @pl.when(cond)
@@ -136,6 +145,9 @@
         for f in range(2, frames + 2):
             when_recv(has_up, row_copy(p, f, True))
             when_recv(has_down, row_copy(p, f, False))
+        for f in (1, 0):
+            when_start(to_core & has_up, corner_copy(p, f, True))
+            when_start(to_core & has_down, corner_copy(p, f, False))
         for o in range(frames):
             contrib(p, o, tuple(t for t in range(3) if o + t >= 2), True)
         if meanwhile is not None:
@@ -143,20 +155,29 @@
         for o in range(2, frames):
             for c in range(chunks):
                 finish(o, c)
-        for f in (1, 0):
+        def arrive(f):
             for c in range(chunks):
                 when_recv(has_prev, time_copy(p, f, c))
                 if c == 0:
-                    when_start(has_prev & has_up, row_copy(p, f, False))
+                    when_start(other_chip & has_up, row_copy(p, f, False))
                 if c == chunks - 1:
-                    when_start(has_prev & has_down, row_copy(p, f, True))
+                    when_start(other_chip & has_down, row_copy(p, f, True))
+
+        def corners(f):
             when_recv(has_prev & has_up, row_copy(p, f, True))
             when_recv(has_prev & has_down, row_copy(p, f, False))
-            for o in range(f, -1, -1):
-                contrib(p, o, (f - o,), False)
-                if o == f:
-                    for c in range(chunks):
-                        finish(o, c)
+
+        arrive(1)
+        corners(1)
+        contrib(p, 1, (0,), False)
+        for c in range(chunks):
+            finish(1, c)
+        arrive(0)
+        contrib(p, 0, (1,), False)
+        corners(0)
+        contrib(p, 0, (0,), False)
+        for c in range(chunks):
+            finish(0, c)
 
     for copy in small:
         copy.wait()
@@ -187,7 +208,6 @@
     load1.wait()
     load2.start()
     turn(0, w1)
-    other_chip = has_prev & (lax.rem(tm, 2) == 0)
 
     def turn_second():
         load2.wait()
@@ -208,8 +228,11 @@
         for f in range(2):
             for c in range(chunks):
                 when_sent(has_next, time_copy(p, f, c))
+        for f in range(2):
+            when_sent(to_core & has_up, corner_copy(p, f, True))
+            when_sent(to_core & has_down, corner_copy(p, f, False))
         for f in range(frames + 2):
-            extra = has_prev if f < 2 else True
+            extra = other_chip if f < 2 else True
             when_sent(has_up & extra, row_copy(p, f, False))
             when_sent(has_down & extra, row_copy(p, f, True))
 
@@ -243,6 +266,7 @@
             dma((2, 2, chunks)),
             dma((2, frames + 2, 2)),
             dma((2, frames + 2, 2)),
+            dma((2, 2, 2)),
         ],
         compiler_params=pltpu.CompilerParams(
             collective_id=0, has_side_effects=True, vmem_limit_bytes=56 * 2**20

time: 48.1 us -> 45.9 us (0.954)
  the two profiles are of different devices: /device:TPU:14 before, /device:TPU:12 now
where the time goes in v4:
time: 45.9 us; the launch traced here: 45.5 us
  Pallas kernels  43.4 us (95%)
  local copies, waits for them, and re-layouts  2.07 us (5%)
    pallas_call x1, Pallas kernels, local(): pl.pallas_call(functools.partial(kernel, tms, heights), out_shape=jax.Sha...  43.4 us
    unnamed x1, local copies, waits for them, and re-layouts  2.07 us

profile of v4, /device:TPU:12, one launch (start us, length us, event | category | flops | bytes accessed | tf_op | source)
XLA Modules:
  0.0 45.5 jit_solution(7036348744186713302)
XLA Ops:
  0.0 43.4 %shard_map.73 = bf16[2,8,192,128]{3,2,1,0:T(8,128)(2,1)} custom-call(bf16[2,8,192,128]{3,2,1,0:T(8,128)(2,1)} %bitcast.7, f32[1,192]{1,0:T(1,128)} %bitcast.8, f32[1,192]{1,0:T(1,128)} %bitcast.9, f32[1,192]{1,0:T(1,128)} %bitcast.10, f32[1,192]{1,0:T(1,128)} %bitcast.11, bf16[3,3,3,192,192]{4,3,2,1,0:T(8,128)(2,1)} %w1_hbm.1, ...), custom_call_target="tpu_custom_call" | custom-call | flops 8153726976 | bytes 8388608 | tf_op jit(solution)/shard_map/pallas_call | solution.py:250
  43.4 2.1 %copy.9 = bf16[2,8,128,192]{2,3,1,0:T(8,128)(2,1)} copy(bf16[2,8,128,192]{2,3,1,0:T(8,128)(2,1)} %bitcast.6) | data formatting | bytes 1572864
